TPU v7x, 32 devices: a whole 2x2x4 slice. The times are simulated.
32 devices in a mesh: outer: 2 (over x), sec: 8 (over z, core), tp: 2 (over y).
Axes of the slice: x: 2, y: 2, z: 4, core: 2. Of those that a mesh axis runs over, the one named last changes fastest.
Arguments:
- tile_maps: bfloat16 [32, 12, 12, 3072], P(('outer', 'sec'), None, None, 'tp'), may hold values from -6 to 6
- tile_shape: int32 [32, 2], P(('outer', 'sec')), may hold values from 4 to 12
- conv_kernel: float32 [7, 7, 3072], P(None, None, 'tp'), may hold values from -0.875 to 0.875
- norm_gain: float32 [3072], P('tp'), may hold values from 0.25 to 1.75
- norm_bias: float32 [3072], P('tp'), may hold values from -3 to 3
- projector: bfloat16 [3072, 7168], P('tp', 'sec'), may hold values from -0.109375 to 0.109375
- text_rows: bfloat16 [9216, 7168], P(('outer', 'sec'), 'tp'), may hold values from -6 to 6
- row_order: int32 [16, 576], P(('outer', 'sec')), may hold values from 0 to 575, each once within a row
- seq_gain: float32 [7168], P('tp'), may hold values from 0.25 to 1.75
- cotangent: bfloat16 [9216, 7168], P(('outer', 'sec'), 'tp'), may hold values from -0.2772166 to 0.2772166, as said below
Outputs:
- normed: bfloat16 [9216, 7168], P(('outer', 'sec'), 'tp')
- kernel_delta: float32 [7, 7, 3072], P(None, None, 'tp')
- gain_delta: float32 [3072], P('tp')
- bias_delta: float32 [3072], P('tp')
Inputs may be any that keep to these rules, and one draw needn't show every extreme that they name: `row_order`: each row lists where the visual tokens arriving at that device stand, in arrival order, then the text rows. `tile_shape`: valid rows and columns of each tile, the rest of the map is padding. `cotangent`: gradient of the training loss.
All inputs are finite; a program needn't handle non-finite values.
Results may differ from a plain program's by a relative error of at most 0.0043.
Values may be sent and summed in bfloat16 or wider, within the bound.
A program may use at most 128 MiB of HBM per device.

v0:
```python
import jax
import jax.numpy as jnp
from jax import lax
from jax.sharding import PartitionSpec as P


def shape_mask(tile_shape, grid):
    places = lax.broadcasted_iota(jnp.int32, (1, grid), 1)
    rows_ok = places < tile_shape[:, 0:1]
    cols_ok = places < tile_shape[:, 1:2]
    return (rows_ok[:, :, None] & cols_ok[:, None, :]).astype(jnp.float32)


def on_device(
    tile_maps,
    tile_shape,
    conv_kernel,
    norm_gain,
    norm_bias,
    projector,
    text_rows,
    row_order,
    seq_gain,
    cotangent,
):
    grid = tile_maps.shape[1]
    half_ch = tile_maps.shape[3]
    channels = half_ch * lax.axis_size("tp")
    rows_dev = tile_maps.shape[0] * grid * grid
    width = text_rows.shape[1] * lax.axis_size("tp")
    validity = shape_mask(tile_shape, grid)[..., None]
    masked = tile_maps.astype(jnp.float32) * validity
    padded = jnp.pad(masked, ((0, 0), (3, 3), (3, 3), (0, 0)))
    conv_out = jnp.zeros(masked.shape, jnp.float32)
    for row_off in range(7):
        for col_off in range(7):
            conv_out = (
                conv_out
                + padded[:, row_off : row_off + grid, col_off : col_off + grid, :]
                * conv_kernel[row_off, col_off]
            )
    total_one, total_two = lax.psum(
        (jnp.sum(conv_out, axis=-1), jnp.sum(conv_out * conv_out, axis=-1)), "tp"
    )
    center = (total_one / channels)[..., None]
    inverse = lax.rsqrt((total_two / channels)[..., None] - center * center + 1e-06)
    normal = (conv_out - center) * inverse
    features = (
        (validity * (normal * norm_gain + norm_bias))
        .astype(jnp.bfloat16)
        .reshape(rows_dev, half_ch)
    )
    whole_weight = lax.all_gather(projector, "sec", axis=1, tiled=True)
    partial_value = jnp.dot(features, whole_weight, preferred_element_type=jnp.float32)
    visual = lax.psum_scatter(partial_value, "tp", scatter_dimension=1, tiled=True).astype(
        jnp.bfloat16
    )
    arrived = lax.all_to_all(visual, "sec", split_axis=0, concat_axis=0, tiled=True)
    positions = row_order[0, :rows_dev]
    merged = text_rows.at[positions].set(arrived)
    wide = merged.astype(jnp.float32)
    upstream = cotangent.astype(jnp.float32) * seq_gain
    square_sum, along = lax.psum(
        (jnp.sum(wide * wide, axis=-1), jnp.sum(upstream * wide, axis=-1)), "tp"
    )
    inv_rms = lax.rsqrt(square_sum / width + 1e-05)[:, None]
    normed = (wide * inv_rms * seq_gain).astype(jnp.bfloat16)
    grad_seq = inv_rms * upstream - wide * (inv_rms * inv_rms * inv_rms) * along[:, None] / width
    picked = grad_seq[positions].astype(jnp.bfloat16)
    returned = lax.all_to_all(picked, "sec", split_axis=0, concat_axis=0, tiled=True)
    full_grad = lax.all_gather(returned, "tp", axis=1, tiled=True)
    grad_rows = jnp.dot(full_grad, whole_weight.T, preferred_element_type=jnp.float32)
    masked_grad = grad_rows.reshape(masked.shape) * validity
    scaled = masked_grad * norm_gain
    first_sum, second_sum = lax.psum(
        (jnp.sum(scaled, axis=-1), jnp.sum(scaled * normal, axis=-1)), "tp"
    )
    grad_conv = inverse * (
        scaled - (first_sum / channels)[..., None] - normal * (second_sum / channels)[..., None]
    )
    kernel_rows = []
    for row_off in range(7):
        for col_off in range(7):
            window = padded[:, row_off : row_off + grid, col_off : col_off + grid, :]
            kernel_rows.append(jnp.sum(window * grad_conv, axis=(0, 1, 2)))
    gain_grad = jnp.sum(masked_grad * normal, axis=(0, 1, 2))
    bias_grad = jnp.sum(masked_grad, axis=(0, 1, 2))
    local_delta = jnp.stack(kernel_rows + [gain_grad, bias_grad], axis=0)
    pods = lax.axis_size("outer")
    entries = 51 * channels
    pod_sum = lax.psum(local_delta, "sec")
    norm_sq = lax.psum(jnp.sum(pod_sum * pod_sum), "tp")
    factor = jnp.minimum(1.0, 1.0 / jnp.sqrt(norm_sq / entries + 1e-06))
    average = lax.psum(pod_sum * factor, "outer") / pods
    return (normed, average[:49].reshape(7, 7, half_ch), average[49], average[50])


def solution(mesh):
    in_specs = (
        P(("outer", "sec"), None, None, "tp"),
        P(("outer", "sec"), None),
        P(None, None, "tp"),
        P("tp"),
        P("tp"),
        P("tp", "sec"),
        P(("outer", "sec"), "tp"),
        P(("outer", "sec"), None),
        P("tp"),
        P(("outer", "sec"), "tp"),
    )
    out_specs = (P(("outer", "sec"), "tp"), P(None, None, "tp"), P("tp"), P("tp"))
    return jax.shard_map(
        on_device, mesh=mesh, in_specs=in_specs, out_specs=out_specs, check_vma=False
    )
```

profile of v0, /device:TPU:0, one launch (start us, length us, event | category | flops | bytes accessed | tf_op | source)
XLA Modules:
  0.0 696.8 jit_solution(15552070662868830435)
XLA Ops:
  7.2 4.4 copy.23
  14.4 23.6 %fusion.8 = (f32[2,12,12]{2,1,0:T(8,128)S(1)}, f32[2,12,12]{2,1,0:T(8,128)S(1)}, f32[2,12,12,1536]{3,2,1,0:T(8,128)}) fusion(f32[1536]{0:T(1024)S(1)} %get-tuple-element.110, f32[1536]{0:T(1024)S(1)} %get-tuple-element.111, f32[1536]{0:T(1024)S(1)} %get-tuple-element.64, f32[1536]{0:T(1024)S(1)} %get-tuple-element.65, f32[1536]{0:T(1024)S(1)} %get-tuple-element.66, ...), kind=kLoop, calls=%fused_computation.189 | loop fusion | flops 44236224 | bytes 3842304 | tf_op jit(solution)/shard_map/reduce_sum | solution.py:43
  38.1 9.8 %all-reduce.3 = (f32[2,12,12]{2,1,0:T(8,128)S(1)}, f32[2,12,12]{2,1,0:T(8,128)S(1)}) all-reduce(f32[2,12,12]{2,1,0:T(8,128)S(1)} %get-tuple-element.58, f32[2,12,12]{2,1,0:T(8,128)S(1)} %get-tuple-element.57), channel_id=1, replica_groups=mesh['outer'=2,'sec'=8,'tp'=2] {'tp'}, use_global_device_ids=true, to_apply=%region_3.4 | all-reduce | flops 576 | bytes 4608 | tf_op jit(solution)/shard_map/psum | solution.py:42
  48.5 3.5 multiply_convert_fusion
  53.1 155.4 %all-gather.3.cloned.1.call-done = bf16[1536,7168]{1,0:T(8,128)(2,1)} async-done(((bf16[1536,896]{1,0:T(8,128)(2,1)}), bf16[1536,7168]{1,0:T(8,128)(2,1)}) %all-gather.3.cloned.1.call-update) | async-done | bytes 22020112 | tf_op jit(solution)/shard_map/all_gather | solution.py:53
  208.5 13.1 %fusion.9 = f32[288,7168]{1,0:T(8,128)} fusion(bf16[288,1536]{1,0:T(8,128)(2,1)} %reshape.168, bf16[1536,7168]{1,0:T(8,128)(2,1)} %all-gather.3.cloned.1.call-done), kind=kOutput, calls=%fused_computation.190 | convolution fusion | flops 6341787648 | bytes 31162368 | tf_op jit(solution)/shard_map/dot_general | solution.py:54
  221.7 96.2 %reduce-scatter.2.cloned.1.call-done = f32[288,3584]{1,0:T(8,128)} async-done(((f32[288,7168]{1,0:T(8,128)}), f32[288,3584]{1,0:T(8,128)}) %reduce-scatter.2.cloned.1.call-update) | async-done | bytes 4128784 | tf_op jit(solution)/shard_map/reduce_scatter | solution.py:55
  317.8 3.7 convert_element_type.43
  321.6 4.0 all_to_all.14
  325.5 4.7 all-to-all-start
  330.5 53.1 %all-to-all-done = bf16[8,36,3584]{2,1,0:T(8,128)(2,1)} async-done(((bf16[8,36,3584]{2,1,0:T(8,128)(2,1)}), bf16[8,36,3584]{2,1,0:T(8,128)(2,1)}, u32[]{:S(2)}, u32[]{:S(2)}) %all-to-all-start) | async-done | bytes 2064416 | tf_op jit(solution)/shard_map/all_to_all | solution.py:58
  383.7 4.0 reshape.184
  387.7 9.2 %scatter_fusion = bf16[576,3584]{1,0:T(8,128)(2,1)} fusion(bf16[576,3584]{1,0:T(8,128)(2,1)} %copy.23, s32[288]{0:T(512)S(1)} %fusion.7, bf16[288,3584]{1,0:T(8,128)(2,1)} %reshape.184), kind=kCustom, calls=%fused_computation.1 | custom fusion | bytes 6194304 | tf_op jit(solution)/shard_map/scatter | solution.py:60
  396.9 5.4 fusion.6
  402.3 5.0 all-reduce.2
  407.3 6.7 fusion.5
  414.0 10.0 %gather_fusion = bf16[288,3584]{1,0:T(8,128)(2,1)} fusion(bf16[576,3584]{1,0:T(8,128)(2,1)} %fusion.5, s32[1024]{0:T(1024)S(1)} %pad_clamp_fusion), kind=kCustom, calls=%fused_computation | custom fusion | bytes 4129920 | tf_op jit(solution)/shard_map/gather | solution.py:69
  424.1 4.0 convert_element_type.48
  428.0 57.6 %all_to_all.21 = bf16[8,36,3584]{2,1,0:T(8,128)(2,1)} all-to-all(bf16[8,36,3584]{2,1,0:T(8,128)(2,1)} %convert_element_type.48), channel_id=1, replica_groups=mesh['outer'=2,'sec'=8,'tp'=2] {'sec'}, dimensions={0} | all-to-all | bytes 4128768 | tf_op jit(solution)/shard_map/all_to_all | solution.py:70
  485.7 4.0 all_to_all.18
  489.8 54.0 %all-gather.5.cloned.1.call-done = bf16[288,7168]{1,0:T(8,128)(2,1)} async-done(((bf16[288,3584]{1,0:T(8,128)(2,1)}), bf16[288,7168]{1,0:T(8,128)(2,1)}) %all-gather.5.cloned.1.call-update) | async-done | bytes 4128784 | tf_op jit(solution)/shard_map/all_gather | solution.py:71
  543.7 13.2 %multiply_reduce_fusion.53 = (f32[1536]{0:T(1024)S(1)}, f32[288]{0:T(512)S(1)}, f32[288,1536]{1,0:T(8,128)}) fusion(f32[288]{0:T(512)S(1)} %reshape.171, f32[1536]{0:T(1024)S(1)} %copy-done.8, bf16[288,7168]{1,0:T(8,128)(2,1)} %all-gather.5.cloned.1.call-done, bf16[1536,7168]{1,0:T(8,128)(2,1)} %all-gather.3.cloned.1.call-done), kind=kOutput, calls=%fused_computation.120 | convolution fusion | flops 6343555072 | bytes 27932928 | tf_op jit(solution)/shard_map/dot_general | solution.py:72
  559.8 3.4 multiply_reduce_fusion
  563.2 7.4 %all-reduce.1 = (f32[2,12,12]{2,1,0:T(8,128)S(1)}, f32[2,12,12]{2,1,0:T(8,128)S(1)}) all-reduce(f32[2,12,12]{2,1,0:T(8,128)S(1)} %get-tuple-element.5, f32[2,12,12]{2,1,0:T(8,128)S(1)} %reduce_sum.529), channel_id=1, replica_groups=mesh['outer'=2,'sec'=8,'tp'=2] {'tp'}, use_global_device_ids=true, to_apply=%region_13.14 | all-reduce | flops 576 | bytes 4608 | tf_op jit(solution)/shard_map/psum | solution.py:75
  570.7 9.6 %multiply_reduce_fusion.1 = (f32[1536]{0:T(1024)S(1)}, f32[1536]{0:T(1024)S(1)}, f32[1536]{0:T(1024)S(1)}, f32[1536]{0:T(1024)S(1)}, f32[1536]{0:T(1024)S(1)}, /...) fusion(f32[2,12,12,1536]{3,2,1,0:T(8,128)S(1)} %convert_multipl, ...), kind=kLoop, calls=%fused_computation.63 | loop fusion | flops 19436544 | bytes 7200384 | tf_op jit(solution)/shard_map/reduce_sum | solution.py:85
  580.3 6.3 multiply_reduce_fusion.19
  586.6 5.4 multiply_reduce_fusion.38
  592.8 4.8 stack.207
  597.7 54.4 %all-reduce.7.cloned.1.call-done = f32[51,1536]{1,0:T(8,128)} async-done(((f32[51,1536]{1,0:T(8,128)}), f32[51,1536]{1,0:T(8,128)}) %all-reduce.7.cloned.1.call-update) | async-done | bytes 313360 | tf_op jit(solution)/shard_map/psum | solution.py:91
  653.7 5.5 psum.70
  661.7 5.5 fusion.2
  667.2 20.6 %all-reduce.9.cloned.1.call-done = f32[51,1536]{1,0:T(8,128)} async-done(((f32[51,1536]{1,0:T(8,128)}), f32[51,1536]{1,0:T(8,128)}) %all-reduce.9.cloned.1.call-update) | async-done | bytes 313360 | tf_op jit(solution)/shard_map/psum | solution.py:94
  (105 shorter events, 14.1 us)
Async XLA Ops:
  7.2 201.4 %all-gather.3.cloned.1.call-start = ((), (), s32[]{:S(2)}) async-start(), calls=%async_computation.3 | async-start | bytes 24772608 | tf_op jit(solution)/shard_map/all_gather | solution.py:53
  11.6 0.7 copy-start.9
  11.6 1.0 copy-start.2
  11.6 2.6 copy-start
  11.7 306.2 %reduce-scatter.2.cloned.1.call-start = ((), (), s32[]{:S(2)}) async-start(), calls=%async_computation.4 | async-start | bytes 12386304 | tf_op jit(solution)/shard_map/reduce_scatter | solution.py:55
  47.9 0.6 copy-start.3
  47.9 0.6 copy-start.5
  325.5 5.0 copy-start.10
  325.5 58.1 %all-to-all-start = ((bf16[8,36,3584]{2,1,0:T(8,128)(2,1)}), bf16[8,36,3584]{2,1,0:T(8,128)(2,1)}, u32[]{:S(2)}, u32[]{:S(2)}) async-start(bf16[8,36,3584]{2,1,0:T(8,128)(2,1)} %all_to_all.14), calls=%async_computation.1 | async-start | bytes 4587520 | tf_op jit(solution)/shard_map/all_to_all | solution.py:58
  330.3 213.5 %all-gather.5.cloned.1.call-start = ((), (), s32[]{:S(2)}) async-start(), calls=%async_computation.5 | async-start | bytes 6193152 | tf_op jit(solution)/shard_map/all_gather | solution.py:71
  387.7 9.2 %copy-start.7 = (f32[3584]{0:T(1024)S(1)}, f32[3584]{0:T(1024)}, u32[]{:S(2)}) copy-start(f32[3584]{0:T(1024)} %param.18) | copy-start | bytes 43012
  485.6 58.1 %copy-start.8 = (f32[1536]{0:T(1024)S(1)}, f32[1536]{0:T(1024)}, u32[]{:S(2)}) copy-start(f32[1536]{0:T(1024)} %param.13) | copy-start | bytes 18436
  489.6 162.4 %all-reduce.7.cloned.1.call-start = ((), (), s32[]{:S(2)}) async-start(), calls=%async_computation.6 | async-start | bytes 688128 | tf_op jit(solution)/shard_map/psum | solution.py:91
  557.0 2.8 copy-start.4
  557.0 2.8 copy-start.6
  580.3 6.4 copy-start.1
  597.6 90.2 %all-reduce.9.cloned.1.call-start = ((), (), s32[]{:S(2)}) async-start(), calls=%async_computation.7 | async-start | bytes 688128 | tf_op jit(solution)/shard_map/psum | solution.py:94
Sparse Core Ops, SparseCore 0:
  11.8 196.7 all-gather.2
  221.8 96.0 reduce-scatter.1
  489.8 53.9 all-gather.4
  597.7 54.2 all-reduce.6
  661.8 25.9 all-reduce.8
where the time goes:
time: 698 us; the launch traced here: 697 us
  waiting for transfers between devices  434 us (62%)
  blocking collectives  85.4 us (12%)
  other arithmetic  78 us (11%)
  local copies, waits for them, and re-layouts  53.2 us (8%)
  matrix products  26.4 us (4%)
  between operations  15 us (2%)
    all_gather x1, waiting for transfers between devices, on_device(): whole_weight = lax.all_gather(projector, 'sec', axis=1, tiled=True)  155 us
    reduce_scatter x1, waiting for transfers between devices, on_device(): lax.psum_scatter(partial_value, 'tp', scatter_dimension=1, tiled=True)  96.2 us
    all_to_all x1, blocking collectives, on_device(): lax.all_to_all(picked, 'sec', split_axis=0, concat_axis=0, tiled=True)  57.6 us
    psum x1, waiting for transfers between devices, on_device(): pod_sum = lax.psum(local_delta, 'sec')  54.4 us
    all_gather x1, waiting for transfers between devices, on_device(): full_grad = lax.all_gather(returned, 'tp', axis=1, tiled=True)  54 us
    all_to_all x1, waiting for transfers between devices, on_device(): lax.all_to_all(visual, 'sec', split_axis=0, concat_axis=0, tiled=True)  53.1 us
    reduce_sum x1, other arithmetic, on_device(): jnp.sum(conv_out, axis=-1)  23.6 us
    reduce_sum x3, other arithmetic, on_device(): kernel_rows.append(jnp.sum(window * grad_conv, axis=(0, 1, 2)))  21.3 us
  transfers between devices with their start and end apart: 6, of which 6 were waited for; matrix products, arithmetic and copies ran while one was open for 5% of the time, Pallas kernels for 0%

commit v1 on v0

--- a/solution.py
+++ b/solution.py
@@ -1,7 +1,16 @@
+import functools
 import jax
 import jax.numpy as jnp
 from jax import lax
 from jax.sharding import PartitionSpec as P
+
+
+def review_knots(tile_in, axis_name):
+    v_now = jax.lax.all_gather(tile_in, axis_name=axis_name)
+    return jnp.sum(v_now, 0)
+
+
+_end_region = functools.partial(review_knots, axis_name="sec")
 
 
 def shape_mask(tile_shape, grid):
@@ -88,7 +97,7 @@
     local_delta = jnp.stack(kernel_rows + [gain_grad, bias_grad], axis=0)
     pods = lax.axis_size("outer")
     entries = 51 * channels
-    pod_sum = lax.psum(local_delta, "sec")
+    pod_sum = _end_region(local_delta)
     norm_sq = lax.psum(jnp.sum(pod_sum * pod_sum), "tp")
     factor = jnp.minimum(1.0, 1.0 / jnp.sqrt(norm_sq / entries + 1e-06))
     average = lax.psum(pod_sum * factor, "outer") / pods

time: 698 us -> 677 us (0.970)
  waiting for transfers between devices: 434 us -> 413 us
    psum x1 -> x0, waiting for transfers between devices: 54.4 us -> none  [on_device(): pod_sum = lax.psum(local_delta, 'sec')]
    all_gather x0 -> x1, waiting for transfers between devices: none -> 36.3 us  [review_knots(): v_now = jax.lax.all_gather(tile_in, axis_name=axis_name)]
where the time goes in v1:
time: 677 us; the launch traced here: 676 us
  waiting for transfers between devices  413 us (61%)
  blocking collectives  85.4 us (13%)
  other arithmetic  78 us (12%)
  local copies, waits for them, and re-layouts  53.2 us (8%)
  matrix products  26.4 us (4%)
  between operations  15 us (2%)
    all_gather x1, waiting for transfers between devices, on_device(): whole_weight = lax.all_gather(projector, 'sec', axis=1, tiled=True)  155 us
    reduce_scatter x1, waiting for transfers between devices, on_device(): lax.psum_scatter(partial_value, 'tp', scatter_dimension=1, tiled=True)  96.2 us
    all_to_all x1, blocking collectives, on_device(): lax.all_to_all(picked, 'sec', split_axis=0, concat_axis=0, tiled=True)  57.6 us
    all_gather x1, waiting for transfers between devices, on_device(): full_grad = lax.all_gather(returned, 'tp', axis=1, tiled=True)  54 us
    all_to_all x1, waiting for transfers between devices, on_device(): lax.all_to_all(visual, 'sec', split_axis=0, concat_axis=0, tiled=True)  53.1 us
    all_gather x1, waiting for transfers between devices, review_knots(): v_now = jax.lax.all_gather(tile_in, axis_name=axis_name)  36.3 us
    reduce_sum x1, other arithmetic, on_device(): jnp.sum(conv_out, axis=-1)  23.6 us
    reduce_sum x3, other arithmetic, on_device(): kernel_rows.append(jnp.sum(window * grad_conv, axis=(0, 1, 2)))  21.3 us
  transfers between devices with their start and end apart: 6, of which 6 were waited for; matrix products, arithmetic and copies ran while one was open for 5% of the time, Pallas kernels for 0%

profile of v1, /device:TPU:0, one launch (start us, length us, event | category | flops | bytes accessed | tf_op | source)
XLA Modules:
  0.0 676.3 jit_solution(6664848680185500515)
XLA Ops:
  7.2 4.4 copy.23
  14.4 23.6 %fusion.8 = (f32[2,12,12]{2,1,0:T(8,128)S(1)}, f32[2,12,12]{2,1,0:T(8,128)S(1)}, f32[2,12,12,1536]{3,2,1,0:T(8,128)}) fusion(f32[1536]{0:T(1024)S(1)} %get-tuple-element.110, f32[1536]{0:T(1024)S(1)} %get-tuple-element.111, f32[1536]{0:T(1024)S(1)} %get-tuple-element.64, f32[1536]{0:T(1024)S(1)} %get-tuple-element.65, f32[1536]{0:T(1024)S(1)} %get-tuple-element.66, ...), kind=kLoop, calls=%fused_computation.189 | loop fusion | flops 44236224 | bytes 3842304 | tf_op jit(solution)/shard_map/reduce_sum | solution.py:52
  38.1 9.8 %all-reduce.3 = (f32[2,12,12]{2,1,0:T(8,128)S(1)}, f32[2,12,12]{2,1,0:T(8,128)S(1)}) all-reduce(f32[2,12,12]{2,1,0:T(8,128)S(1)} %get-tuple-element.58, f32[2,12,12]{2,1,0:T(8,128)S(1)} %get-tuple-element.57), channel_id=1, replica_groups=mesh['outer'=2,'sec'=8,'tp'=2] {'tp'}, use_global_device_ids=true, to_apply=%region_3.4 | all-reduce | flops 576 | bytes 4608 | tf_op jit(solution)/shard_map/psum | solution.py:51
  48.5 3.5 multiply_convert_fusion
  53.1 155.4 %all-gather.6.cloned.1.call-done = bf16[1536,7168]{1,0:T(8,128)(2,1)} async-done(((bf16[1536,896]{1,0:T(8,128)(2,1)}), bf16[1536,7168]{1,0:T(8,128)(2,1)}) %all-gather.6.cloned.1.call-update) | async-done | bytes 22020112 | tf_op jit(solution)/shard_map/all_gather | solution.py:62
  208.5 13.1 %fusion.9 = f32[288,7168]{1,0:T(8,128)} fusion(bf16[288,1536]{1,0:T(8,128)(2,1)} %reshape.168, bf16[1536,7168]{1,0:T(8,128)(2,1)} %all-gather.6.cloned.1.call-done), kind=kOutput, calls=%fused_computation.190 | convolution fusion | flops 6341787648 | bytes 31162368 | tf_op jit(solution)/shard_map/dot_general | solution.py:63
  221.7 96.2 %reduce-scatter.2.cloned.1.call-done = f32[288,3584]{1,0:T(8,128)} async-done(((f32[288,7168]{1,0:T(8,128)}), f32[288,3584]{1,0:T(8,128)}) %reduce-scatter.2.cloned.1.call-update) | async-done | bytes 4128784 | tf_op jit(solution)/shard_map/reduce_scatter | solution.py:64
  317.8 3.7 convert_element_type.43
  321.6 4.0 all_to_all.14
  325.5 4.7 all-to-all-start
  330.5 53.1 %all-to-all-done = bf16[8,36,3584]{2,1,0:T(8,128)(2,1)} async-done(((bf16[8,36,3584]{2,1,0:T(8,128)(2,1)}), bf16[8,36,3584]{2,1,0:T(8,128)(2,1)}, u32[]{:S(2)}, u32[]{:S(2)}) %all-to-all-start) | async-done | bytes 2064416 | tf_op jit(solution)/shard_map/all_to_all | solution.py:67
  383.7 4.0 reshape.184
  387.7 9.2 %scatter_fusion = bf16[576,3584]{1,0:T(8,128)(2,1)} fusion(bf16[576,3584]{1,0:T(8,128)(2,1)} %copy.23, s32[288]{0:T(512)S(1)} %fusion.7, bf16[288,3584]{1,0:T(8,128)(2,1)} %reshape.184), kind=kCustom, calls=%fused_computation.1 | custom fusion | bytes 6194304 | tf_op jit(solution)/shard_map/scatter | solution.py:69
  396.9 5.4 fusion.6
  402.3 5.0 all-reduce.2
  407.3 6.7 fusion.5
  414.0 10.0 %gather_fusion = bf16[288,3584]{1,0:T(8,128)(2,1)} fusion(bf16[576,3584]{1,0:T(8,128)(2,1)} %fusion.5, s32[1024]{0:T(1024)S(1)} %pad_clamp_fusion), kind=kCustom, calls=%fused_computation | custom fusion | bytes 4129920 | tf_op jit(solution)/shard_map/gather | solution.py:78
  424.1 4.0 convert_element_type.48
  428.0 57.6 %all_to_all.21 = bf16[8,36,3584]{2,1,0:T(8,128)(2,1)} all-to-all(bf16[8,36,3584]{2,1,0:T(8,128)(2,1)} %convert_element_type.48), channel_id=1, replica_groups=mesh['outer'=2,'sec'=8,'tp'=2] {'sec'}, dimensions={0} | all-to-all | bytes 4128768 | tf_op jit(solution)/shard_map/all_to_all | solution.py:79
  485.7 4.0 all_to_all.18
  489.8 54.0 %all-gather.8.cloned.1.call-done = bf16[288,7168]{1,0:T(8,128)(2,1)} async-done(((bf16[288,3584]{1,0:T(8,128)(2,1)}), bf16[288,7168]{1,0:T(8,128)(2,1)}) %all-gather.8.cloned.1.call-update) | async-done | bytes 4128784 | tf_op jit(solution)/shard_map/all_gather | solution.py:80
  543.7 13.2 %multiply_reduce_fusion.53 = (f32[1536]{0:T(1024)S(1)}, f32[288]{0:T(512)S(1)}, f32[288,1536]{1,0:T(8,128)}) fusion(f32[288]{0:T(512)S(1)} %reshape.171, f32[1536]{0:T(1024)S(1)} %copy-done.8, bf16[288,7168]{1,0:T(8,128)(2,1)} %all-gather.8.cloned.1.call-done, bf16[1536,7168]{1,0:T(8,128)(2,1)} %all-gather.6.cloned.1.call-done), kind=kOutput, calls=%fused_computation.120 | convolution fusion | flops 6343555072 | bytes 27932928 | tf_op jit(solution)/shard_map/dot_general | solution.py:81
  559.8 3.4 multiply_reduce_fusion
  563.2 7.4 %all-reduce.1 = (f32[2,12,12]{2,1,0:T(8,128)S(1)}, f32[2,12,12]{2,1,0:T(8,128)S(1)}) all-reduce(f32[2,12,12]{2,1,0:T(8,128)S(1)} %get-tuple-element.5, f32[2,12,12]{2,1,0:T(8,128)S(1)} %reduce_sum.538), channel_id=1, replica_groups=mesh['outer'=2,'sec'=8,'tp'=2] {'tp'}, use_global_device_ids=true, to_apply=%region_13.14 | all-reduce | flops 576 | bytes 4608 | tf_op jit(solution)/shard_map/psum | solution.py:84
  570.7 9.6 %multiply_reduce_fusion.1 = (f32[1536]{0:T(1024)S(1)}, f32[1536]{0:T(1024)S(1)}, f32[1536]{0:T(1024)S(1)}, f32[1536]{0:T(1024)S(1)}, f32[1536]{0:T(1024)S(1)}, /...) fusion(f32[2,12,12,1536]{3,2,1,0:T(8,128)S(1)} %convert_multipl, ...), kind=kLoop, calls=%fused_computation.63 | loop fusion | flops 19436544 | bytes 7200384 | tf_op jit(solution)/shard_map/reduce_sum | solution.py:94
  580.3 6.3 multiply_reduce_fusion.19
  586.6 5.4 multiply_reduce_fusion.38
  592.8 4.8 stack.207
  597.7 36.3 %all-gather.10.cloned.1.call-done = f32[8,51,1536]{2,1,0:T(8,128)} async-done(((f32[1,51,1536]{2,1,0:T(8,128)}), f32[8,51,1536]{2,1,0:T(8,128)}) %all-gather.10.cloned.1.call-update) | async-done | bytes 2506768 | tf_op jit(solution)/shard_map/all_gather | solution.py:9
  636.6 5.5 psum.62
  643.6 5.5 fusion.2
  649.2 18.2 %all-reduce.6.cloned.1.call-done = f32[51,1536]{1,0:T(8,128)} async-done(((f32[51,1536]{1,0:T(8,128)}), f32[51,1536]{1,0:T(8,128)}) %all-reduce.6.cloned.1.call-update) | async-done | bytes 313360 | tf_op jit(solution)/shard_map/psum | solution.py:103
  (106 shorter events, 14.1 us)
Async XLA Ops:
  7.2 201.4 %all-gather.6.cloned.1.call-start = ((), (), s32[]{:S(2)}) async-start(), calls=%async_computation.3 | async-start | bytes 24772608 | tf_op jit(solution)/shard_map/all_gather | solution.py:62
  11.6 0.7 copy-start.9
  11.6 1.0 copy-start.2
  11.6 2.6 copy-start
  11.7 306.2 %reduce-scatter.2.cloned.1.call-start = ((), (), s32[]{:S(2)}) async-start(), calls=%async_computation.4 | async-start | bytes 12386304 | tf_op jit(solution)/shard_map/reduce_scatter | solution.py:64
  47.9 0.6 copy-start.3
  47.9 0.6 copy-start.5
  325.5 5.0 copy-start.10
  325.5 58.1 %all-to-all-start = ((bf16[8,36,3584]{2,1,0:T(8,128)(2,1)}), bf16[8,36,3584]{2,1,0:T(8,128)(2,1)}, u32[]{:S(2)}, u32[]{:S(2)}) async-start(bf16[8,36,3584]{2,1,0:T(8,128)(2,1)} %all_to_all.14), calls=%async_computation.1 | async-start | bytes 4587520 | tf_op jit(solution)/shard_map/all_to_all | solution.py:67
  330.3 213.5 %all-gather.8.cloned.1.call-start = ((), (), s32[]{:S(2)}) async-start(), calls=%async_computation.5 | async-start | bytes 6193152 | tf_op jit(solution)/shard_map/all_gather | solution.py:80
  387.7 9.2 %copy-start.7 = (f32[3584]{0:T(1024)S(1)}, f32[3584]{0:T(1024)}, u32[]{:S(2)}) copy-start(f32[3584]{0:T(1024)} %param.18) | copy-start | bytes 43012
  485.6 58.1 %copy-start.8 = (f32[1536]{0:T(1024)S(1)}, f32[1536]{0:T(1024)}, u32[]{:S(2)}) copy-start(f32[1536]{0:T(1024)} %param.13) | copy-start | bytes 18436
  489.6 144.3 %all-gather.10.cloned.1.call-start = ((), (), s32[]{:S(2)}) async-start(), calls=%async_computation.7 | async-start | bytes 3096576 | tf_op jit(solution)/shard_map/all_gather | solution.py:9
  557.0 2.8 copy-start.4
  557.0 2.8 copy-start.6
  580.3 6.4 copy-start.1
  597.6 69.8 %all-reduce.6.cloned.1.call-start = ((), (), s32[]{:S(2)}) async-start(), calls=%async_computation.6 | async-start | bytes 688128 | tf_op jit(solution)/shard_map/psum | solution.py:103
Sparse Core Ops, SparseCore 0:
  11.8 196.7 all-gather.5
  221.8 96.0 reduce-scatter.1
  489.8 53.9 all-gather.7
  597.7 36.1 all-gather.9
  643.7 23.5 all-reduce.5
